TPU v7x, 32 devices: a whole 2x2x4 slice. The times are simulated.
32 devices in a mesh: expert: 4 (over y, core), shard: 8 (over z, x).
Axes of the slice: x: 2, y: 2, z: 4, core: 2. Of those that a mesh axis runs over, the one named last changes fastest.
Arguments:
- tokens: bfloat16 [16384, 1024], P(('expert', 'shard')), may hold values from -6 to 6
- cotangent: bfloat16 [16384, 1024], P(('expert', 'shard')), may hold values from -6 to 6
- routes: int32 [16384, 8], P(('expert', 'shard')), may hold values from 0 to 31, all different within a row; in each aligned block of 512 rows (0 to 511, 512 to 1023, ...) at most 256 rows name the same one
- segments: int32 [32, 512], P(('expert', 'shard')), may hold values from 0 to 7, never falling along the last dimension, each value on 1 to 256 neighbouring positions
- tile_counts: int32 [32, 32], P(('expert', 'shard')), may hold values from 1 to 2
- norm1_gain: bfloat16 [1024], P('shard'), may hold values from 0.5 to 1.5
- w_query: bfloat16 [1024, 1024], P('shard'), may hold values from -0.1875 to 0.1875
- w_key: bfloat16 [1024, 512], P('shard'), may hold values from -0.1875 to 0.1875
- w_value: bfloat16 [1024, 512], P('shard'), may hold values from -0.1875 to 0.1875
- w_out: bfloat16 [1024, 1024], P('shard'), may hold values from -0.75 to 0.75
- norm2_gain: bfloat16 [1024], P('shard'), may hold values from 0.5 to 1.5
- w_router: bfloat16 [1024, 32], P('shard'), may hold values from -0.1875 to 0.1875
- w_gate_up: bfloat16 [32, 1024, 1024], P('expert', 'shard'), may hold values from -0.1875 to 0.1875
- w_down: bfloat16 [32, 512, 1024], P('expert', 'shard'), may hold values from -0.75 to 0.75
Outputs:
- output: bfloat16 [16384, 1024], P(('expert', 'shard'))
- grad_tokens: float32 [16384, 1024], P(('expert', 'shard'))
- grad_norm1: float32 [1024], P('shard')
- grad_query: float32 [1024, 1024], P('shard')
- grad_key: float32 [1024, 512], P('shard')
- grad_value: float32 [1024, 512], P('shard')
- grad_out: float32 [1024, 1024], P('shard')
- grad_norm2: float32 [1024], P('shard')
- grad_router: float32 [1024, 32], P('shard')
- grad_gate_up: float32 [32, 1024, 1024], P('expert', 'shard')
- grad_down: float32 [32, 512, 1024], P('expert', 'shard')
Inputs may be any that keep to these rules, and one draw needn't show every extreme that they name: `routes`: each token names 8 different experts; among the tokens of one sequence no expert is named more than 256 times. `segments`: never falling along a sequence; every document number of a sequence is used, each by at most half of 512 positions.
All inputs are finite; a program needn't handle non-finite values.
Results may differ from a plain program's by a relative error of at most 0.015.
Values may be sent and summed in bfloat16 or wider, within the bound.
A program may use at most 320 MiB of HBM per device.

v0:
```python
import jax
import jax.numpy as jnp
from jax import lax
from jax.sharding import PartitionSpec as P

D = 1024
H = 16
KVH = 8
HD = 64
FF = 512
EXPERTS = 32
TOP = 8
TILE = 128
CAP = 256


EPSILON = 1e-06
ROTARY_BASE = 10000.0
MASKED = -1e30


def rotary_tables(length, head_size):
    halfway = head_size // 2
    exponent = jnp.arange(halfway, dtype=jnp.float32) * (2.0 / head_size)
    angles = jnp.arange(length, dtype=jnp.float32)[:, None] * (ROTARY_BASE ** (-exponent))[None, :]
    cosine = jnp.concatenate([jnp.cos(angles), jnp.cos(angles)], -1)
    sine = jnp.concatenate([jnp.sin(angles), jnp.sin(angles)], -1)
    return (cosine, sine)


def rotate(values, cosine, sine):
    halfway = values.shape[-1] // 2
    turned = jnp.concatenate([-values[..., halfway:], values[..., :halfway]], -1)
    return values * cosine[:, None, :] + turned * sine[:, None, :]


def masked_scores(query_low, key_low, allowed):
    scores = jnp.einsum(
        "qkgd,tkd->kgqt", query_low, key_low, preferred_element_type=jnp.float32
    ) * HD ** (-0.5)
    return jnp.where(allowed[None, None], scores, MASKED)


def local(
    tokens,
    cotangent,
    routes,
    segments,
    tile_counts,
    norm1_gain,
    w_query,
    w_key,
    w_value,
    w_out,
    norm2_gain,
    w_router,
    w_gate_up,
    w_down,
):
    length = tokens.shape[0]
    groups = H // KVH
    highest = lax.Precision.HIGHEST
    (
        gain_first,
        query_weight,
        key_weight,
        value_weight,
        output_weight,
        gain_second,
        router_weight,
    ) = (
        lax.all_gather(norm1_gain, "shard", axis=0, tiled=True),
        lax.all_gather(w_query, "shard", axis=0, tiled=True),
        lax.all_gather(w_key, "shard", axis=0, tiled=True),
        lax.all_gather(w_value, "shard", axis=0, tiled=True),
        lax.all_gather(w_out, "shard", axis=0, tiled=True),
        lax.all_gather(norm2_gain, "shard", axis=0, tiled=True),
        lax.all_gather(w_router, "shard", axis=0, tiled=True),
    )
    joined_weight, down_weight = (
        lax.all_gather(w_gate_up, "shard", axis=1, tiled=True),
        lax.all_gather(w_down, "shard", axis=1, tiled=True),
    )
    holders = lax.axis_size("expert")
    local_count = joined_weight.shape[0]
    inputs = tokens.astype(jnp.float32)
    scale_first = lax.rsqrt(jnp.mean(inputs * inputs, -1, keepdims=True) + EPSILON)
    gain_one = gain_first.astype(jnp.float32)
    normed_low = (inputs * scale_first * gain_one).astype(jnp.bfloat16)
    cosine, sine = rotary_tables(length, HD)
    query_raw = jnp.dot(normed_low, query_weight, preferred_element_type=jnp.float32).reshape(
        length, H, HD
    )
    query_low = (
        rotate(query_raw, cosine, sine).astype(jnp.bfloat16).reshape(length, KVH, groups, HD)
    )
    key_raw = jnp.dot(normed_low, key_weight, preferred_element_type=jnp.float32).reshape(
        length, KVH, HD
    )
    key_low = rotate(key_raw, cosine, sine).astype(jnp.bfloat16)
    value_low = (
        jnp.dot(normed_low, value_weight, preferred_element_type=jnp.float32)
        .astype(jnp.bfloat16)
        .reshape(length, KVH, HD)
    )
    document = segments[0]
    places = jnp.arange(length)
    allowed = (document[:, None] == document[None, :]) & (places[:, None] >= places[None, :])
    scores = masked_scores(query_low, key_low, allowed)
    row_max = jnp.max(scores, -1, keepdims=True)
    log_total = row_max + jnp.log(jnp.sum(jnp.exp(scores - row_max), -1, keepdims=True))
    probs_low = jnp.exp(scores - log_total).astype(jnp.bfloat16)
    attended = jnp.einsum(
        "kgqt,tkd->qkgd", probs_low, value_low, preferred_element_type=jnp.float32
    )
    attended_low = attended.astype(jnp.bfloat16).reshape(length, H * HD)
    residual = inputs + jnp.dot(attended_low, output_weight, preferred_element_type=jnp.float32)
    scale_second = lax.rsqrt(jnp.mean(residual * residual, -1, keepdims=True) + EPSILON)
    gain_two = gain_second.astype(jnp.float32)
    mixed_low = (residual * scale_second * gain_two).astype(jnp.bfloat16)
    logits = jnp.dot(mixed_low, router_weight, preferred_element_type=jnp.float32)
    onehot = (routes[:, :, None] == jnp.arange(EXPERTS, dtype=jnp.int32)[None, None, :]).astype(
        jnp.int32
    )
    onehot_float = onehot.astype(jnp.float32)
    chosen = jnp.sum(logits[:, None, :] * onehot_float, -1)
    chosen_exp = jnp.exp(chosen - jnp.max(chosen, -1, keepdims=True))
    gating = chosen_exp / jnp.sum(chosen_exp, -1, keepdims=True)
    flat_hot = onehot.reshape(length * TOP, EXPERTS)
    ranking = jnp.sum((jnp.cumsum(flat_hot, 0) - flat_hot) * flat_hot, -1)
    limits = TILE * jnp.sum(flat_hot * tile_counts[0][None, :], -1)
    kept = ranking < limits
    placed = routes.reshape(-1) * CAP + ranking
    target = jnp.where(kept, placed, EXPERTS * CAP)
    pickup = jnp.minimum(placed, EXPERTS * CAP - 1)
    owners = jnp.arange(length * TOP) // TOP
    kept_float = kept.astype(jnp.float32)[:, None]
    outgoing = (
        jnp.zeros((EXPERTS * CAP, D), jnp.bfloat16).at[target].set(mixed_low[owners], mode="drop")
    )
    outgoing = outgoing.reshape(holders, local_count, CAP, D)
    incoming = lax.all_to_all(outgoing, "expert", split_axis=0, concat_axis=0, tiled=True)
    joined = jnp.einsum(
        "sdcm,dmf->sdcf", incoming, joined_weight, preferred_element_type=jnp.float32
    )
    gate_pre = joined[..., :FF]
    up_pre = joined[..., FF:]
    sigmoid_gate = jax.nn.sigmoid(gate_pre)
    activated = gate_pre * sigmoid_gate
    hidden_low = (activated * up_pre).astype(jnp.bfloat16)
    expert_low = jnp.einsum(
        "sdcf,dfm->sdcm", hidden_low, down_weight, preferred_element_type=jnp.float32
    ).astype(jnp.bfloat16)
    returned = lax.all_to_all(
        expert_low, "expert", split_axis=0, concat_axis=0, tiled=True
    ).reshape(EXPERTS * CAP, D)
    picked = (returned[pickup].astype(jnp.float32) * kept_float).reshape(length, TOP, D)
    output = (residual + jnp.sum(gating[:, :, None] * picked, 1)).astype(jnp.bfloat16)
    upstream = cotangent.astype(jnp.float32)
    slot_grad = (gating.reshape(-1)[:, None] * upstream[owners]).astype(jnp.bfloat16)
    outgoing_grad = (
        jnp.zeros((EXPERTS * CAP, D), jnp.bfloat16).at[target].set(slot_grad, mode="drop")
    )
    outgoing_grad = outgoing_grad.reshape(holders, local_count, CAP, D)
    gating_grad = jnp.sum(upstream[:, None, :] * picked, -1)
    chosen_grad = gating * (gating_grad - jnp.sum(gating * gating_grad, -1, keepdims=True))
    logits_grad = jnp.sum(chosen_grad[:, :, None] * onehot_float, 1)
    router_grad = jnp.dot(mixed_low.astype(jnp.float32).T, logits_grad, precision=highest)
    mixed_grad = jnp.dot(logits_grad, router_weight.astype(jnp.float32).T, precision=highest)
    incoming_grad = lax.all_to_all(outgoing_grad, "expert", split_axis=0, concat_axis=0, tiled=True)
    hidden_grad = jnp.einsum(
        "sdcm,dfm->sdcf", incoming_grad, down_weight, preferred_element_type=jnp.float32
    )
    down_grad = jnp.einsum(
        "sdcf,sdcm->dfm", hidden_low, incoming_grad, preferred_element_type=jnp.float32
    )
    gate_grad = hidden_grad * up_pre * sigmoid_gate * (1.0 + gate_pre * (1.0 - sigmoid_gate))
    up_grad = hidden_grad * activated
    joined_grad = jnp.concatenate([gate_grad, up_grad], -1).astype(jnp.bfloat16)
    input_slots = jnp.einsum(
        "sdcf,dmf->sdcm", joined_grad, joined_weight, preferred_element_type=jnp.float32
    ).astype(jnp.bfloat16)
    joined_weight_grad = jnp.einsum(
        "sdcm,sdcf->dmf", incoming, joined_grad, preferred_element_type=jnp.float32
    )
    returned_grad = lax.all_to_all(
        input_slots, "expert", split_axis=0, concat_axis=0, tiled=True
    ).reshape(EXPERTS * CAP, D)
    mixed_grad = mixed_grad + jnp.sum(
        (returned_grad[pickup].astype(jnp.float32) * kept_float).reshape(length, TOP, D), 1
    )
    gained_two = gain_two * mixed_grad
    gain_two_grad = jnp.sum(mixed_grad * residual * scale_second, 0)
    residual_grad = (
        upstream
        + scale_second * gained_two
        - residual * scale_second**3 * jnp.mean(gained_two * residual, -1, keepdims=True)
    )
    branch_low = residual_grad.astype(jnp.bfloat16)
    output_weight_grad = jnp.einsum(
        "sn,sm->nm", attended_low, branch_low, preferred_element_type=jnp.float32
    )
    attended_grad = jnp.einsum(
        "sm,nm->sn", branch_low, output_weight, preferred_element_type=jnp.float32
    )
    attended_grad = attended_grad.astype(jnp.bfloat16).reshape(length, KVH, groups, HD)
    probs = jnp.exp(masked_scores(query_low, key_low, allowed) - log_total)
    probs_again = probs.astype(jnp.bfloat16)
    value_grad = jnp.einsum(
        "kgqt,qkgd->tkd", probs_again, attended_grad, preferred_element_type=jnp.float32
    )
    probs_grad = jnp.einsum(
        "qkgd,tkd->kgqt", attended_grad, value_low, preferred_element_type=jnp.float32
    )
    scores_grad = (probs * (probs_grad - jnp.sum(probs * probs_grad, -1, keepdims=True))).astype(
        jnp.bfloat16
    )
    query_grad = jnp.einsum(
        "kgqt,tkd->qkgd", scores_grad, key_low, preferred_element_type=jnp.float32
    ).reshape(length, H, HD) * HD ** (-0.5)
    key_grad = jnp.einsum(
        "kgqt,qkgd->tkd", scores_grad, query_low, preferred_element_type=jnp.float32
    ) * HD ** (-0.5)
    query_back = rotate(query_grad, cosine, -sine).astype(jnp.bfloat16).reshape(length, H * HD)
    key_back = rotate(key_grad, cosine, -sine).astype(jnp.bfloat16).reshape(length, KVH * HD)
    value_back = value_grad.astype(jnp.bfloat16).reshape(length, KVH * HD)
    query_weight_grad = jnp.einsum(
        "sm,sn->mn", normed_low, query_back, preferred_element_type=jnp.float32
    )
    key_weight_grad = jnp.einsum(
        "sm,sn->mn", normed_low, key_back, preferred_element_type=jnp.float32
    )
    value_weight_grad = jnp.einsum(
        "sm,sn->mn", normed_low, value_back, preferred_element_type=jnp.float32
    )
    normed_grad = jnp.einsum(
        "sn,mn->sm", query_back, query_weight, preferred_element_type=jnp.float32
    )
    normed_grad = normed_grad + jnp.einsum(
        "sn,mn->sm", key_back, key_weight, preferred_element_type=jnp.float32
    )
    normed_grad = normed_grad + jnp.einsum(
        "sn,mn->sm", value_back, value_weight, preferred_element_type=jnp.float32
    )
    gained_one = gain_one * normed_grad
    gain_one_grad = jnp.sum(normed_grad * inputs * scale_first, 0)
    token_grad = (
        residual_grad
        + scale_first * gained_one
        - inputs * scale_first**3 * jnp.mean(gained_one * inputs, -1, keepdims=True)
    )
    totals = (
        gain_one_grad,
        query_weight_grad,
        key_weight_grad,
        value_weight_grad,
        output_weight_grad,
        gain_two_grad,
        router_grad,
    )
    summed = lax.psum(
        (totals[0], totals[1], totals[2], totals[3], totals[4], totals[5], totals[6]),
        ("expert", "shard"),
    )
    member = lax.axis_index("shard")
    parts = lax.axis_size("shard")
    shares = tuple(
        (
            lax.dynamic_slice_in_dim(
                total, member * (total.shape[0] // parts), total.shape[0] // parts, 0
            )
            for total in summed
        )
    )
    joined_share, down_share = (
        lax.psum_scatter(
            joined_weight_grad.astype(jnp.bfloat16), "shard", scatter_dimension=1, tiled=True
        ).astype(jnp.float32),
        lax.psum_scatter(
            down_grad.astype(jnp.bfloat16), "shard", scatter_dimension=1, tiled=True
        ).astype(jnp.float32),
    )
    return (
        output,
        token_grad,
        shares[0],
        shares[1],
        shares[2],
        shares[3],
        shares[4],
        shares[5],
        shares[6],
        joined_share,
        down_share,
    )


def solution(mesh):
    in_specs = (
        P(("expert", "shard"), None),
        P(("expert", "shard"), None),
        P(("expert", "shard"), None),
        P(("expert", "shard"), None),
        P(("expert", "shard"), None),
        P("shard"),
        P("shard", None),
        P("shard", None),
        P("shard", None),
        P("shard", None),
        P("shard"),
        P("shard", None),
        P("expert", "shard", None),
        P("expert", "shard", None),
    )
    out_specs = (
        P(("expert", "shard"), None),
        P(("expert", "shard"), None),
        P("shard"),
        P("shard", None),
        P("shard", None),
        P("shard", None),
        P("shard", None),
        P("shard"),
        P("shard", None),
        P("expert", "shard", None),
        P("expert", "shard", None),
    )
    return jax.shard_map(local, mesh=mesh, in_specs=in_specs, out_specs=out_specs, check_vma=False)
```

profile of v0, /device:TPU:0, one launch (start us, length us, event | category | flops | bytes accessed | tf_op | source)
XLA Modules:
  0.0 1940.3 jit_solution(9581971091277640560)
XLA Ops:
  11.7 22.3 %all-gather = bf16[8,1,128]{2,1,0:T(2,128)(2,1)S(1)} all-gather(bf16[1,1,128]{2,1,0:T(2,128)(2,1)} %bitcast.232), channel_id=1, replica_groups=mesh['expert'=4,'shard'=8] {'shard'}, dimensions={0}, use_global_device_ids=true | all-gather | bytes 2304 | tf_op jit(solution)/shard_map/all_gather | solution.py:72
  34.0 16.5 all-gather.1
  51.7 9.2 reduce-window.6
  66.2 2.1 fusion.97
  68.7 25.6 %all-gather.9.cloned.1.call-done = bf16[1024,512]{1,0:T(8,128)(2,1)} async-done(((bf16[128,512]{1,0:T(8,128)(2,1)}), bf16[1024,512]{1,0:T(8,128)(2,1)}) %all-gather.9.cloned.1.call-update) | async-done | bytes 1048592 | tf_op jit(solution)/shard_map/all_gather | solution.py:75
  94.3 2.1 convolution_convert_fusion.1
  96.4 48.1 %all-gather.13.cloned.1.call-done = bf16[1024,1024]{1,0:T(8,128)(2,1)} async-done(((bf16[128,1024]{1,0:T(8,128)(2,1)}), bf16[1024,1024]{1,0:T(8,128)(2,1)}) %all-gather.13.cloned.1.call-update) | async-done | bytes 2097168 | tf_op jit(solution)/shard_map/all_gather | solution.py:73
  144.5 3.0 fusion.95
  148.5 7.7 fusion.101
  156.1 8.2 exponential_reduce_fusion
  165.0 8.4 fusion.61
  173.5 20.8 %all-gather.15.cloned.1.call-done = bf16[1024,1024]{1,0:T(8,128)(2,1)} async-done(((bf16[128,1024]{1,0:T(8,128)(2,1)}), bf16[1024,1024]{1,0:T(8,128)(2,1)}) %all-gather.15.cloned.1.call-update) | async-done | bytes 2097168 | tf_op jit(solution)/shard_map/all_gather | solution.py:76
  194.3 3.0 multiply_reduce_fusion.2
  198.8 57.9 %scatter_custom_fusion = bf16[8192,1024]{1,0:T(8,128)(2,1)} fusion(s32[4096]{0:T(1024)S(1)} %bitcast.229, bf16[512,1024]{1,0:T(8,128)(2,1)S(1)} %multiply_convert_fusion.3, s32[4096]{0:T(1024)S(1)} %broadcast_clamp_fusion.1, bf16[]{:T(256)} %constant.21.clone.1), kind=kCustom, calls=%fused_computation.54 | custom fusion | bytes 16777218 | tf_op jit(solution)/shard_map/scatter | solution.py:139
  256.8 7.1 all-to-all-start
  264.5 182.5 %all-to-all-done = bf16[4,8,256,1024]{3,2,1,0:T(8,128)(2,1)} async-done(((bf16[4,8,256,1024]{3,2,1,0:T(8,128)(2,1)}), bf16[4,8,256,1024]{3,2,1,0:T(8,128)(2,1)}, u32[]{:S(2)}, u32[]{:S(2)}) %all-to-all-start) | async-done | bytes 16777248 | tf_op jit(solution)/shard_map/all_to_all | solution.py:142
  446.9 30.8 %fusion.26 = f32[4,8,256,1024]{3,2,0,1:T(8,128)} fusion(bf16[8,1024,1024]{2,1,0:T(8,128)(2,1)} %all-gather.17.cloned.1.call-done, bf16[4,8,256,1024]{3,2,1,0:T(8,128)(2,1)} %all-to-all-done), kind=kOutput, calls=%fused_computation.50 | convolution fusion | flops 17179869184 | bytes 67108864 | tf_op jit(solution)/shard_map/sdcm,dmf->sdcf/dot_general | solution.py:143
  477.7 15.1 multiply_convert_fusion.1
  492.8 54.8 %all-gather.19.cloned.1.call-done = bf16[8,512,1024]{2,1,0:T(8,128)(2,1)} async-done(((bf16[8,64,1024]{2,1,0:T(8,128)(2,1)}), bf16[8,512,1024]{2,1,0:T(8,128)(2,1)}) %all-gather.19.cloned.1.call-update) | async-done | bytes 8388624 | tf_op jit(solution)/shard_map/all_gather | solution.py:82
  547.6 17.0 convert_bitcast_fusion.2
  564.6 13.9 copy.83
  578.5 7.1 all-to-all-start.1
  585.7 1.5 convert_element_type.163
  587.1 26.4 %all_gather.33 = bf16[1024,32]{0,1:T(8,128)(2,1)S(1)} all-gather(bf16[128,32]{0,1:T(8,128)(2,1)S(1)} %copy-done.40), channel_id=1, replica_groups=mesh['expert'=4,'shard'=8] {'shard'}, dimensions={0}, use_global_device_ids=true | all-gather | bytes 73728 | tf_op jit(solution)/shard_map/all_gather | solution.py:78
  614.3 154.4 %all-to-all-done.1 = bf16[4,8,256,1024]{3,2,1,0:T(8,128)(2,1)} async-done(((bf16[4,8,256,1024]{3,2,1,0:T(8,128)(2,1)}), bf16[4,8,256,1024]{3,2,1,0:T(8,128)(2,1)}, u32[]{:S(2)}, u32[]{:S(2)}) %all-to-all-start.1) | async-done | bytes 16777248 | tf_op jit(solution)/shard_map/all_to_all | solution.py:154
  768.7 28.7 %gather_fusion = bf16[4096,1024]{1,0:T(8,128)(2,1)} fusion(bf16[8192,1024]{1,0:T(8,128)(2,1)} %bitcast.31, s32[4096]{0:T(1024)S(1)} %broadcast_clamp_fusion), kind=kCustom, calls=%fused_computation.1 | custom fusion | bytes 16793600 | tf_op jit(solution)/shard_map/gather | solution.py:157
  797.4 5.5 fusion.4
  803.5 49.0 %scatter_custom_fusion.1 = bf16[8192,1024]{1,0:T(8,128)(2,1)} fusion(s32[4096]{0:T(1024)S(1)} %bitcast.230, f32[4096]{0:T(1024)S(1)} %div.54, bf16[]{:T(256)} %constant.21.clone.1, f32[512,1024]{1,0:T(8,128)S(1)} %convert_element_type.163, s32[4096]{0:T(1024)S(1)} %broadcast_clamp_fusion.1), kind=kCustom, calls=%fused_computation.51 | custom fusion | flops 8388608 | bytes 18907138 | tf_op jit(solution)/shard_map/scatter | solution.py:162
  852.4 194.1 %all_to_all.20 = bf16[4,8,256,1024]{3,2,1,0:T(8,128)(2,1)} all-to-all(bf16[4,8,256,1024]{3,2,1,0:T(8,128)(2,1)} %bitcast.188), channel_id=1, replica_groups=mesh['expert'=4,'shard'=8] {'expert'}, dimensions={0} | all-to-all | bytes 33554432 | tf_op jit(solution)/shard_map/all_to_all | solution.py:170
  1046.5 27.5 %fusion.15 = (bf16[4,8,256,512]{3,2,0,1:T(8,128)(2,1)}, bf16[4,8,256,512]{3,2,0,1:T(8,128)(2,1)}) fusion(f32[4,8,256,1024]{3,2,0,1:T(8,128)} %fusion.26, bf16[8,512,1024]{2,1,0:T(8,128)(2,1)} %all-gather.19.cloned.1.call-done, bf16[4,8,256,1024]{3,2,1,0:T(8,128)(2,1)} %all_to_all.20), kind=kOutput, calls=%fused_computation.31 | convolution fusion | flops 8644460544 | bytes 75497472 | tf_op jit(solution)/shard_map/sdcm,dfm->sdcf/dot_general | solution.py:171
  1074.0 24.1 %convert_bitcast_fusion.1 = bf16[4,8,256,1024]{3,2,0,1:T(8,128)(2,1)} fusion(bf16[8,1024,1024]{2,1,0:T(8,128)(2,1)} %all-gather.17.cloned.1.call-done, bf16[4,8,256,512]{3,2,0,1:T(8,128)(2,1)} %get-tuple-element.29, bf16[4,8,256,512]{3,2,0,1:T(8,128)(2,1)} %get-tuple-element.28), kind=kOutput, calls=%fused_computation.37 | convolution fusion | flops 17221812224 | bytes 50331648 | tf_op jit(solution)/shard_map/sdcf,dmf->sdcm/dot_general | solution.py:180
  1098.1 13.9 copy.88
  1112.0 7.0 all-to-all-start.3
  1119.0 15.8 bitcast_convert_fusion.1
  1137.3 164.7 %all-to-all-done.3 = bf16[4,8,256,1024]{3,2,1,0:T(8,128)(2,1)} async-done(((bf16[4,8,256,1024]{3,2,1,0:T(8,128)(2,1)}), bf16[4,8,256,1024]{3,2,1,0:T(8,128)(2,1)}, u32[]{:S(2)}, u32[]{:S(2)}) %all-to-all-start.3) | async-done | bytes 16777248 | tf_op jit(solution)/shard_map/all_to_all | solution.py:186
  1302.0 28.8 %gather_fusion.1 = bf16[4096,1024]{1,0:T(8,128)(2,1)} fusion(bf16[8192,1024]{1,0:T(8,128)(2,1)} %bitcast.40, s32[4096]{0:T(1024)S(1)} %broadcast_clamp_fusion), kind=kCustom, calls=%fused_computation.3 | custom fusion | bytes 16793600 | tf_op jit(solution)/shard_map/gather | solution.py:190
  1330.9 13.5 fusion.5
  1344.4 1.7 multiply_reduce_fusion
  1346.2 1.7 multiply_subtract_fusion
  1349.2 2.3 convolution_convert_fusion
  1351.5 1.5 copy.89
  1353.0 15.2 fusion.6
  1369.4 8.7 fusion.8
  1378.2 1.5 bitcast_multiply_fusion.4
  1380.0 1.5 copy-done
  1381.9 1.6 fusion.60
  1383.4 6.0 broadcast_multiply_fusion
  1390.6 3.6 fusion.67
  1394.4 2.2 fusion.89
  1396.6 3.3 fusion.91
  1399.9 4.7 fusion.93
  1404.6 3.3 fusion.79
  1408.0 25.2 %bitcast_convert_fusion = bf16[8,1024,1024]{2,1,0:T(8,128)(2,1)} fusion(bf16[4,8,256,1024]{3,2,1,0:T(8,128)(2,1)} %all-to-all-done, bf16[4,8,256,512]{3,2,0,1:T(8,128)(2,1)} %get-tuple-element.29, bf16[4,8,256,512]{3,2,0,1:T(8,128)(2,1)} %get-tuple-element.28), kind=kOutput, calls=%fused_computation.6 | convolution fusion | flops 17221812224 | bytes 50331648 | tf_op jit(solution)/shard_map/sdcm,sdcf->dmf/dot_general | solution.py:183
  1434.3 2.0 fusion.104
  1436.3 3.3 fusion.103
  1439.6 2.5 fusion.56
  1442.1 39.2 %all-reduce = (f32[1024]{0:T(1024)S(1)}, f32[1024]{0:T(1024)S(1)}) all-reduce(f32[1024]{0:T(1024)S(1)} %get-tuple-element.13, f32[1024]{0:T(1024)S(1)} %get-tuple-element.11), channel_id=1, replica_groups=mesh['expert'=4,'shard'=8] {'expert','shard'}, use_global_device_ids=true, to_apply=%region_22.23 | all-reduce | flops 2048 | bytes 16384 | tf_op jit(solution)/shard_map/psum | solution.py:261
  1482.4 4.2 fusion.53
  1486.7 2.8 convert_element_type.180
  1489.4 154.3 %all-reduce.4.cloned.1.call-done = (f32[1024,1024]{1,0:T(8,128)}, f32[1024,512]{1,0:T(8,128)}, f32[1024,512]{1,0:T(8,128)}, f32[1024,1024]{1,0:T(8,128)}, f32[1024,32]{0,1:T(8,128)}) async-done(((f32[1024,1024]{1,0:T(8,128)}, f32[1024,512]{1,0:T(8,128)}, f32[1024,512]{1,0:T(8,128)}, f32[1024,1024]{1,0:T(8,128)}, f32[1024,32]{0,1:T(8,128)}), (f32[1024,1024]{1,0:T(8,128)}, f32[1024,512]{1,0:T(8,128)}, ...) | async-done | bytes 12714000 | tf_op jit(solution)/shard_map/psum | solution.py:261
  1645.1 1.9 constant_dynamic-slice_fusion.2
  1647.0 2.3 constant_dynamic-slice_fusion.1
  1649.2 280.3 %reduce-scatter.3.cloned.1.call-done = bf16[8,128,1024]{2,1,0:T(8,128)(2,1)} async-done(((bf16[8,1024,1024]{2,1,0:T(8,128)(2,1)}), bf16[8,128,1024]{2,1,0:T(8,128)(2,1)}) %reduce-scatter.3.cloned.1.call-update) | async-done | bytes 2097168 | tf_op jit(solution)/shard_map/reduce_scatter | solution.py:276
  1929.5 4.1 convert_element_type.178
  (166 shorter events, 26.7 us)
Async XLA Ops:
  7.2 57.8 %copy-start.1 = (bf16[512,1024]{1,0:T(8,128)(2,1)S(1)}, bf16[512,1024]{1,0:T(8,128)(2,1)}, u32[]{:S(2)}) copy-start(bf16[512,1024]{1,0:T(8,128)(2,1)} %param.14) | copy-start | bytes 3145732
  7.2 58.7 %copy-start.37 = (s32[1,512]{1,0:T(1,128)S(1)}, s32[1,512]{1,0:T(1,128)}, u32[]{:S(2)}) copy-start(s32[1,512]{1,0:T(1,128)} %param.17) | copy-start | bytes 6148
  7.2 59.0 %all-gather.11.cloned.1.call-start = ((), (), s32[]{:S(2)}) async-start(), calls=%async_computation.7 | async-start | bytes 1179648 | tf_op jit(solution)/shard_map/all_gather | solution.py:74
  7.9 86.4 %all-gather.9.cloned.1.call-start = ((), (), s32[]{:S(2)}) async-start(), calls=%async_computation.6 | async-start | bytes 1179648 | tf_op jit(solution)/shard_map/all_gather | solution.py:75
  8.7 135.8 %all-gather.13.cloned.1.call-start = ((), (), s32[]{:S(2)}) async-start(), calls=%async_computation.8 | async-start | bytes 2359296 | tf_op jit(solution)/shard_map/all_gather | solution.py:73
  9.4 184.9 %all-gather.15.cloned.1.call-start = ((), (), s32[]{:S(2)}) async-start(), calls=%async_computation.9 | async-start | bytes 2359296 | tf_op jit(solution)/shard_map/all_gather | solution.py:76
  10.0 436.9 %all-gather.17.cloned.1.call-start = ((), (), s32[]{:S(2)}) async-start(), calls=%async_computation.10 | async-start | bytes 18874368 | tf_op jit(solution)/shard_map/all_gather | solution.py:81
  34.0 110.5 %copy-start.29 = (f32[8,1,128]{2,1,0:T(1,128)}, f32[8,1,128]{2,1,0:T(1,128)S(1)}, u32[]{:S(2)}) copy-start(f32[8,1,128]{2,1,0:T(1,128)S(1)} %convert_element_type.183) | copy-start | bytes 12292
  50.6 147.3 %copy-start.31 = (f32[8,1,128]{2,1,0:T(1,128)}, f32[8,1,128]{2,1,0:T(1,128)S(1)}, u32[]{:S(2)}) copy-start(f32[8,1,128]{2,1,0:T(1,128)S(1)} %convert_element_type.184) | copy-start | bytes 12292
  65.8 81.7 %copy-start.33 = (f32[512]{0:T(512)}, f32[512]{0:T(512)S(1)}, u32[]{:S(2)}) copy-start(f32[512]{0:T(512)S(1)} %get-tuple-element.47) | copy-start | bytes 6148
  68.7 79.8 %copy-start.13 = (bf16[512,8,64,1]{0,2,3,1:T(8,128)(2,1)}, bf16[512,8,64,1]{0,2,3,1:T(8,128)(2,1)S(1)}, u32[]{:S(2)}) copy-start(bf16[512,8,64,1]{0,2,3,1:T(8,128)(2,1)S(1)} %fusion.75) | copy-start | bytes 1572868
  96.4 68.1 %copy-start.17 = (bf16[512,512]{0,1:T(8,128)(2,1)}, bf16[512,512]{0,1:T(8,128)(2,1)S(1)}, u32[]{:S(2)}) copy-start(bf16[512,512]{0,1:T(8,128)(2,1)S(1)} %convolution_convert_fusion.1) | copy-start | bytes 1572868
  148.5 7.7 copy-start.5
  164.4 0.6 copy-start.23
  173.4 83.3 %copy-start.9 = (bf16[8,64,2,512]{3,1,2,0:T(8,128)(2,1)}, bf16[8,64,2,512]{3,1,2,0:T(8,128)(2,1)S(1)}, u32[]{:S(2)}) copy-start(bf16[8,64,2,512]{3,1,2,0:T(8,128)(2,1)S(1)} %fusion.61) | copy-start | bytes 3145732
  197.2 1.3 copy-start.3
  197.9 58.8 %copy-start.35 = (f32[512]{0:T(512)}, f32[512]{0:T(512)S(1)}, u32[]{:S(2)}) copy-start(f32[512]{0:T(512)S(1)} %get-tuple-element.49) | copy-start | bytes 6148
  198.8 414.7 %copy-start.11 = (bf16[512,1024]{1,0:T(8,128)(2,1)}, bf16[512,1024]{1,0:T(8,128)(2,1)S(1)}, u32[]{:S(2)}) copy-start(bf16[512,1024]{1,0:T(8,128)(2,1)S(1)} %multiply_convert_fusion.3) | copy-start | bytes 3145732
  256.8 190.2 %all-to-all-start = ((bf16[4,8,256,1024]{3,2,1,0:T(8,128)(2,1)}), bf16[4,8,256,1024]{3,2,1,0:T(8,128)(2,1)}, u32[]{:S(2)}, u32[]{:S(2)}) async-start(bf16[4,8,256,1024]{3,2,1,0:T(8,128)(2,1)} %bitcast.187), calls=%async_computation | async-start | bytes 33554432 | tf_op jit(solution)/shard_map/all_to_all | solution.py:142
  263.9 283.8 %all-gather.19.cloned.1.call-start = ((), (), s32[]{:S(2)}) async-start(), calls=%async_computation.11 | async-start | bytes 9437184 | tf_op jit(solution)/shard_map/all_gather | solution.py:82
  578.5 8.6 copy-start.40
  578.5 35.6 %copy-start.27 = (s32[512,8]{0,1:T(8,128)S(1)}, s32[512,8]{0,1:T(8,128)}, u32[]{:S(2)}) copy-start(s32[512,8]{0,1:T(8,128)} %param.16) | copy-start | bytes 49156
  578.5 190.2 %all-to-all-start.1 = ((bf16[4,8,256,1024]{3,2,1,0:T(8,128)(2,1)}), bf16[4,8,256,1024]{3,2,1,0:T(8,128)(2,1)}, u32[]{:S(2)}, u32[]{:S(2)}) async-start(bf16[4,8,256,1024]{3,2,1,0:T(8,128)(2,1)} %copy.83), calls=%async_computation.1 | async-start | bytes 33554432 | tf_op jit(solution)/shard_map/all_to_all | solution.py:154
  613.5 0.6 copy-start.25
  1112.0 190.1 %all-to-all-start.3 = ((bf16[4,8,256,1024]{3,2,1,0:T(8,128)(2,1)}), bf16[4,8,256,1024]{3,2,1,0:T(8,128)(2,1)}, u32[]{:S(2)}, u32[]{:S(2)}) async-start(bf16[4,8,256,1024]{3,2,1,0:T(8,128)(2,1)} %copy.88), calls=%async_computation.3 | async-start | bytes 33554432 | tf_op jit(solution)/shard_map/all_to_all | solution.py:186
  1119.0 367.7 %reduce-scatter.5.cloned.1.call-start = ((), (), s32[]{:S(2)}) async-start(), calls=%async_computation.13 | async-start | bytes 9437184 | tf_op jit(solution)/shard_map/reduce_scatter | solution.py:279
  1134.8 0.7 copy-start.28
  1134.8 1.2 copy-start.12
  1134.8 508.9 %all-reduce.4.cloned.1.call-start = ((), (), s32[]{:S(2)}) async-start(), calls=%async_computation.14 | async-start | bytes 25427968 | tf_op jit(solution)/shard_map/psum | solution.py:261
  1330.8 13.6 copy-start.4
  1330.8 13.6 copy-start.26
  1330.8 13.6 copy-start.32
  1330.8 13.6 copy-start.36
  1330.8 15.3 copy-start.16
  1330.9 15.3 copy-start.39
  1344.4 4.8 copy-start.19
  1346.1 6.9 copy-start.18
  1346.1 6.9 copy-start.24
  1347.9 1.3 copy-start.7
  1353.0 15.2 slice-start
  1353.0 15.2 slice-start.1
  1353.0 15.2 slice-start.2
  1353.0 16.4 slice-start.3
  1369.4 8.7 copy-start.14
  1378.2 3.3 copy-start
  1378.2 3.3 copy-start.20
  1378.2 3.6 copy-start.21
  1379.7 3.7 copy-start.6
  1390.6 3.7 copy-start.2
  1390.6 3.7 copy-start.30
  1390.6 3.7 copy-start.34
  1394.3 10.3 copy-start.8
  1394.3 10.2 copy-start.10
  1407.9 521.6 %reduce-scatter.3.cloned.1.call-start = ((), (), s32[]{:S(2)}) async-start(), calls=%async_computation.12 | async-start | bytes 18874368 | tf_op jit(solution)/shard_map/reduce_scatter | solution.py:276
  1433.2 1.0 copy-start.15
  1433.2 6.3 copy-start.22
  1436.3 46.1 %copy-start.38 = (f32[512]{0:T(512)S(1)}, f32[512]{0:T(512)}, u32[]{:S(2)}) copy-start(f32[512]{0:T(512)} %get-tuple-element.46) | copy-start | bytes 6148
Sparse Core Ops, SparseCore 0:
  10.2 42.9 all-gather.10
  55.3 38.9 all-gather.8
  96.4 48.0 all-gather.12
  146.5 47.7 all-gather.14
  196.3 226.1 all-gather.16
  424.5 123.0 all-gather.18
  1134.9 147.6 reduce-scatter.4
  1408.1 235.6 all-reduce.3
  1648.0 281.4 reduce-scatter.2
where the time goes:
time: 1950 us; the launch traced here: 1940 us
  waiting for transfers between devices  1090 us (56%)
  blocking collectives  298 us (15%)
  matrix products  220 us (11%)
  local copies, waits for them, and re-layouts  161 us (8%)
  other arithmetic  135 us (7%)
  starting transfers between devices  21.8 us (1%)
    reduce_scatter x1, waiting for transfers between devices, local(): lax.psum_scatter(joined_weight_grad.astype(jnp.bfloat16), 'shard', scatte...  280 us
    all_to_all x1, blocking collectives, local(): lax.all_to_all(outgoing_grad, 'expert', split_axis=0, concat_axis=0, tile...  194 us
    all_to_all x1, waiting for transfers between devices, local(): lax.all_to_all(outgoing, 'expert', split_axis=0, concat_axis=0, tiled=True)  182 us
    all_to_all x1, waiting for transfers between devices, local(): lax.all_to_all(input_slots, 'expert', split_axis=0, concat_axis=0, tiled=...  165 us
    all_to_all x1, waiting for transfers between devices, local(): lax.all_to_all(expert_low, 'expert', split_axis=0, concat_axis=0, tiled=T...  154 us
    psum x1, waiting for transfers between devices, local(): lax.psum((totals[0], totals[1], totals[2], totals[3], totals[4], totals[5...  154 us
    scatter x1, local copies, waits for them, and re-layouts, local(): jnp.zeros((EXPERTS * CAP, D), jnp.bfloat16).at[target]  57.9 us
    all_gather x1, waiting for transfers between devices, local(): lax.all_gather(w_down, 'shard', axis=1, tiled=True)  54.8 us
  transfers between devices with their start and end apart: 12, of which 9 were waited for; matrix products, arithmetic and copies ran while one was open for 17% of the time, Pallas kernels for 0%

commit v1 on v0

v1 whole, which is shorter than its diff:
```python
import functools

import jax
import jax.numpy as jnp
from jax import lax
from jax.experimental import pallas as pl
from jax.experimental.pallas import tpu as pltpu
from jax.sharding import PartitionSpec as P

D = 1024
H = 16
KVH = 8
HD = 64
FF = 512
EXPERTS = 32
TOP = 8
TILE = 128
CAP = 256
PLANE = 8
QKV = H * HD + 2 * KVH * HD
PACKED = QKV + D + 128

EPSILON = 1e-06
ROTARY_BASE = 10000.0
MASKED = -1e30

BF = jnp.bfloat16
F32 = jnp.float32
HBM = pl.BlockSpec(memory_space=pltpu.HBM)
VMEM = pl.BlockSpec(memory_space=pltpu.VMEM)
DMA = pltpu.SemaphoreType.DMA
LIMIT = 62 * 1024 * 1024 - 512 * 1024


def dot(a, b):
    return jnp.dot(a, b, preferred_element_type=F32)


def dot_nt(a, b):
    return lax.dot_general(a, b, (((1,), (1,)), ((), ())), preferred_element_type=F32)


def dot_tn(a, b):
    return lax.dot_general(a, b, (((0,), (0,)), ((), ())), preferred_element_type=F32)


def flip(value, bit):
    return value + bit * (1 - 2 * ((value // bit) % 2))


class Sizes:
    def __init__(self, mesh):
        self.holders = mesh.shape["expert"]
        self.shards = mesh.shape["shard"]
        self.f = PLANE // self.holders
        self.n = self.shards // self.f
        self.experts = EXPERTS // PLANE
        self.rows = D // self.shards
        self.rows_down = FF // self.shards
        self.parts = min(self.holders, self.rows // 16)
        self.part = self.rows // self.parts
        self.piece = self.f * (self.rows + self.rows_down)


class Here:
    def __init__(self, t):
        self.t = t
        self.e = lax.axis_index("expert")
        self.idx = lax.axis_index("shard")
        self.r = self.idx // t.f
        self.sub = self.idx % t.f
        self.g = self.e * t.f + self.sub
        self.core = t.f
        self.b1, self.b2 = [b for b in (1, 2, 4) if b != t.f]
        self.pc = flip(self.g, self.core)
        self.p1 = flip(self.g, self.b1)
        self.p2 = flip(self.g, self.b2)
        self.pd = flip(self.p1, self.b2)
        self.mate = flip(self.g, 1)

    def dev(self, g, r=None):
        r = self.r if r is None else r
        return {"expert": g // self.t.f, "shard": r * self.t.f + g % self.t.f}

    def member(self, m):
        g = self.g
        for b in (1, 2, 4):
            if m & b:
                g = flip(g, b)
        return g

    def barrier(self, plane=True, line=True):
        t, r = self.t, self.r
        sem = pltpu.get_barrier_semaphore()
        count = 0
        if plane:
            for m in range(1, PLANE):
                signal(sem, self.dev(self.member(m)))
            count = PLANE - 1
        if line:
            first, last = r == 0, r == t.n - 1
            pl.when(jnp.logical_not(first))(lambda: signal(sem, self.dev(self.g, r - 1)))
            pl.when(jnp.logical_not(last))(lambda: signal(sem, self.dev(self.g, r + 1)))
            pl.when(first | last)(lambda: pl.semaphore_wait(sem, count + 1))
            pl.when(jnp.logical_not(first | last))(lambda: pl.semaphore_wait(sem, count + 2))
        else:
            pl.semaphore_wait(sem, count)


def signal(sem, device):
    pl.semaphore_signal(sem, inc=1, device_id=device, device_id_type=pl.DeviceIdType.MESH)


def remote(src, dst, send, recv, device):
    return pltpu.make_async_remote_copy(
        src_ref=src,
        dst_ref=dst,
        send_sem=send,
        recv_sem=recv,
        device_id=device,
        device_id_type=pl.DeviceIdType.MESH,
    )


class LineGather:
    def __init__(self, here, blk, ss, rs):
        self.h, self.blk, self.ss, self.rs = here, blk, ss, rs

    def copy(self, p, way, r):
        return remote(self.blk(p), self.blk(p), self.ss(way, p), self.rs(p), self.h.dev(self.h.g, r))

    def step(self, s):
        h, n = self.h, self.h.t.n
        r = h.r

        def right():
            c = self.copy(r - s, 0, r + 1)
            if s:
                c.wait_recv()
            c.start()

        def left():
            c = self.copy(r + s, 1, r - 1)
            if s:
                c.wait_recv()
            c.start()

        pl.when((r >= s) & (r < n - 1))(right)
        pl.when((r + s <= n - 1) & (r > 0))(left)

    def fin(self):
        h, n = self.h, self.h.t.n
        r = h.r
        for p in range(n):
            c = self.copy(p, 0, r)
            pl.when(((r > p) & (r == n - 1)) | ((r < p) & (r == 0)))(c.wait_recv)

    def drain(self):
        h, n = self.h, self.h.t.n
        r = h.r
        for s in range(n - 1):
            pl.when((r >= s) & (r < n - 1))(lambda: self.copy(r - s, 0, r + 1).wait_send())
            pl.when((r + s <= n - 1) & (r > 0))(lambda: self.copy(r + s, 1, r - 1).wait_send())


class PlaneGather:
    COUNT = 9

    def __init__(self, here, blk, half, ss, rs, own=None, ok=None):
        h = here
        own = blk(h.g) if own is None else own
        self.ok = ok
        self.ss, self.rs, self.h = ss, rs, h
        self.out = [
            (own, blk(h.g), h.pc, h.g),
            (own, blk(h.g), h.p1, h.g),
            (own, blk(h.g), h.p2, h.g),
            (half(h.p1, 0), half(h.p1, 0), h.p2, h.p1),
            (half(h.p2, 1), half(h.p2, 1), h.p1, h.p2),
            (blk(h.p1), blk(h.p1), h.pc, h.p1),
            (blk(h.p2), blk(h.p2), h.pc, h.p2),
            (half(h.pd, 0), half(h.pd, 0), h.pc, h.pd),
            (half(h.pd, 1), half(h.pd, 1), h.pc, h.pd),
        ]
        c1, c2 = flip(h.pc, h.b1), flip(h.pc, h.b2)
        cd = flip(c1, h.b2)
        self.arrive = [
            (blk(h.pc), h.pc),
            (blk(h.p1), h.p1),
            (blk(h.p2), h.p2),
            (half(h.pd, 0), h.pd),
            (half(h.pd, 1), h.pd),
            (blk(c1), c1),
            (blk(c2), c2),
            (half(cd, 0), cd),
            (half(cd, 1), cd),
        ]

    def guard(self, origin, fn):
        if self.ok is None:
            fn()
        else:
            pl.when(self.ok(origin))(fn)

    def make(self, i):
        src, dst, peer, origin = self.out[i]
        return remote(src, dst, self.ss(i), self.rs(i), self.h.dev(peer)), origin

    def send(self, *which):
        for i in which:
            c, origin = self.make(i)
            self.guard(origin, c.start)

    def wait(self, *which):
        for i in which:
            dst, origin = self.arrive[i]
            c = remote(dst, dst, self.ss(i), self.rs(i), self.h.dev(self.h.pc))
            self.guard(origin, c.wait_recv)

    def start(self):
        self.send(1, 2, 0)

    def second(self):
        self.wait(1)
        self.send(3, 5)
        self.wait(2)
        self.send(4, 6)

    def third(self):
        self.wait(3)
        self.send(7)
        self.wait(4)
        self.send(8)

    def fin(self):
        self.wait(0, 5, 6, 7, 8)

    def drain(self):
        for i in range(self.COUNT):
            c, origin = self.make(i)
            self.guard(origin, c.wait_send)


class Mates:
    def __init__(self, here, pairs, ss, rs):
        self.h, self.pairs, self.ss, self.rs = here, pairs, ss, rs

    def copies(self, el):
        return [
            (remote(src, there, self.ss(el, k), self.rs(el, k), self.h.dev(self.h.mate)),
             remote(mine, mine, self.ss(el, k), self.rs(el, k), self.h.dev(self.h.mate)))
            for k, (src, there, mine) in enumerate(self.pairs(el))
        ]

    def start(self, el):
        if self.h.t.f > 1:
            for c, _ in self.copies(el):
                c.start()

    def wait(self, el):
        if self.h.t.f > 1:
            for _, c in self.copies(el):
                c.wait_recv()

    def drain(self, el):
        if self.h.t.f > 1:
            for c, _ in self.copies(el):
                c.wait_send()


def rope(block, cosine, sine_a, sine_b):
    return block * cosine + pltpu.roll(block, 96, 1) * sine_a + pltpu.roll(block, 32, 1) * sine_b


def first_kernel(
    t,
    x_ref, routes_ref, doc_row_ref, doc_col_ref, counts_ref, cos_ref, sin_a_ref, sin_b_ref,
    g_in, packed_in, gu_in, down_in,
    w_out, ga_out, h2_out, info_out, packed_out, res_ref, att_ref, q_ref, k_ref, v_ref, p_out, gate_ref,
    aw, bias, p_stage, h2_stage, info_stage, loc, one_s, one_r, aw_ls, aw_lr, aw_ps, aw_pr,
    mate_s, mate_r, w_ls, w_lr, g_ps, g_pr, h_ps, h_pr, i_s, i_r, p_sem,
):
    h = Here(t)
    n, r, sub, E = t.n, h.r, h.sub, t.experts
    q = h.e % t.parts
    h.barrier()

    def awb(g, *rest):
        return aw.at[:, g % t.f, (g // t.f) % t.parts]

    ok = None if t.parts == t.holders else (lambda g: g // t.f < t.parts)
    half_rows = PACKED // 2 // 128 * 128

    def aw_half(g, k):
        lo, size = ((0, half_rows), (half_rows, PACKED - half_rows))[k]
        return aw.at[:, g % t.f, (g // t.f) % t.parts, :, pl.ds(lo, size)]

    gu_rows = lambda s: pl.ds(s * t.rows, t.rows)
    down_rows = lambda s: pl.ds(t.f * t.rows + s * t.rows_down, t.rows_down)

    own = [
        pltpu.make_async_copy(packed_in.at[pl.ds(q * t.part, t.part)], aw.at[r, sub, q], loc.at[0]),
        pltpu.make_async_copy(gu_in.at[pl.ds(sub * E, E)], w_out.at[:, r, gu_rows(sub)], loc.at[1]),
        pltpu.make_async_copy(down_in.at[pl.ds(sub * E, E)], w_out.at[:, r, down_rows(sub)], loc.at[2]),
        pltpu.make_async_copy(g_in, ga_out.at[h.g], loc.at[3]),
    ]
    for c in own:
        c.start()
    other = t.f - 1 - sub
    mates = Mates(
        h,
        lambda el: [
            (gu_in.at[other * E + el], w_out.at[el, r, gu_rows(sub)], w_out.at[el, r, gu_rows(other)]),
            (down_in.at[other * E + el], w_out.at[el, r, down_rows(sub)], w_out.at[el, r, down_rows(other)]),
        ],
        lambda el, k: mate_s.at[el, k],
        lambda el, k: mate_r.at[el, k],
    )
    mates.start(0)
    mates.start(1)
    line_a = LineGather(h, lambda p: aw.at[p, sub, q], lambda way, p: aw_ls.at[way, p], lambda p: aw_lr.at[p])
    lines = [
        LineGather(
            h,
            lambda p, el=el: w_out.at[el, p],
            lambda way, p, el=el: w_ls.at[el, way, p],
            lambda p, el=el: w_lr.at[el, p],
        )
        for el in range(E)
    ]
    plane_a = PlaneGather(h, awb, aw_half, lambda i: aw_ps.at[i], lambda i: aw_pr.at[i], ok=ok)
    rows_half = lambda ref: (lambda g, k: ref.at[g, pl.ds(k * 256, 256)])
    plane_g = PlaneGather(
        h, lambda g: ga_out.at[g], rows_half(ga_out), lambda i: g_ps.at[i], lambda i: g_pr.at[i], own=g_in
    )
    plane_h = PlaneGather(
        h, lambda g: h2_out.at[g], rows_half(h2_out), lambda i: h_ps.at[i], lambda i: h_pr.at[i], own=h2_stage
    )
    own[0].wait()
    for s in range(n - 1):
        line_a.step(s)
    line_a.fin()
    plane_a.start()
    own[1].wait()
    own[2].wait()
    for el in (0, 1):
        mates.wait(el)
        lines[el].step(0)
    mates.start(2)
    mates.start(3)

    length = x_ref.shape[0]
    same = doc_col_ref[...] == doc_row_ref[...]
    before = lax.broadcasted_iota(jnp.int32, (length, length), 0) >= lax.broadcasted_iota(
        jnp.int32, (length, length), 1
    )
    bias[...] = jnp.where(same & before, 0.0, MASKED)
    expert_rows = lax.broadcasted_iota(jnp.int32, (EXPERTS, length), 0)
    routed = jnp.zeros((EXPERTS, length), F32)
    for k in range(TOP):
        routed = routed + jnp.where(expert_rows == routes_ref[k : k + 1, :], 1.0, 0.0)
    earlier = jnp.where(
        lax.broadcasted_iota(jnp.int32, (length, length), 0) < lax.broadcasted_iota(jnp.int32, (length, length), 1),
        1.0,
        0.0,
    ).astype(BF)
    rank = dot(routed.astype(BF), earlier)
    kept = (routed > 0.5) & (rank < counts_ref[...] * float(TILE))
    slot = jnp.where(kept, rank, -1.0)

    plane_a.second()
    plane_a.third()
    plane_a.fin()
    for s in range(1, n - 1):
        lines[0].step(s)
    plane_g.start()
    own[3].wait()
    keep = pltpu.make_async_copy(aw, packed_out, loc.at[4])
    keep.start()

    tail = aw[:, :, :, :, QKV + D : PACKED].reshape(D, PACKED - QKV - D).astype(F32).T
    gain_one, gain_two = tail[EXPERTS : EXPERTS + 1, :], tail[EXPERTS + 1 : EXPERTS + 2, :]
    x = x_ref[...].astype(F32)
    scale = lax.rsqrt(jnp.mean(x * x, -1, keepdims=True) + EPSILON)
    a1 = (x * scale * gain_one).astype(BF)
    cosine, sine_a, sine_b = cos_ref[...], sin_a_ref[...], sin_b_ref[...]
    weight = lambda lo, hi: aw[:, :, :, :, lo:hi].reshape(D, hi - lo)
    for c in range(2):
        block = dot(a1, weight(c * 512, c * 512 + 512))
        for b in range(4):
            q_ref[4 * c + b] = rope(block[:, b * 128 : b * 128 + 128], cosine, sine_a, sine_b).astype(BF)
    block = dot(a1, weight(H * HD, H * HD + KVH * HD))
    for b in range(4):
        turned = rope(block[:, b * 128 : b * 128 + 128], cosine, sine_a, sine_b).astype(BF)
        k_ref[2 * b] = turned[:, :HD]
        k_ref[2 * b + 1] = turned[:, HD:]
    block = dot(a1, weight(H * HD + KVH * HD, QKV)).astype(BF)
    for b in range(KVH):
        v_ref[b] = block[:, b * HD : b * HD + HD]
    for s in range(1, n - 1):
        lines[1].step(s)
    for el in (2, 3):
        mates.wait(el)
        lines[el].step(0)

    def heads(b, carry):
        pair = q_ref[b]
        stacked = jnp.concatenate([pair[:, :HD], pair[:, HD:]], 0)
        scores = dot_nt(stacked, k_ref[b]) * HD ** (-0.5)
        scores = scores.reshape(2, length, length) + bias[...][None]
        top = jnp.max(scores, -1, keepdims=True)
        raised = jnp.exp(scores - top)
        total = jnp.sum(raised, -1, keepdims=True)
        probs = (raised / total).astype(BF).reshape(2 * length, length)

        @pl.when(b >= 2)
        def _():
            pltpu.make_async_copy(p_stage.at[b % 2], p_out.at[b], p_sem.at[b % 2]).wait()

        p_stage[b % 2] = probs
        pltpu.make_async_copy(p_stage.at[b % 2], p_out.at[b], p_sem.at[b % 2]).start()
        mixed = dot(probs, v_ref[b]).astype(BF)
        att_ref[:, pl.ds(pl.multiple_of(b * 128, 128), 128)] = jnp.concatenate(
            [mixed[:length], mixed[length:]], 1
        )
        return carry

    lax.fori_loop(0, KVH, heads, 0)
    for b in range(2):
        pltpu.make_async_copy(p_stage.at[b], p_out.at[b], p_sem.at[b]).wait()
    plane_g.second()

    residual = x + dot(att_ref[...], weight(QKV, QKV + D))
    res_ref[...] = residual
    scale_two = lax.rsqrt(jnp.mean(residual * residual, -1, keepdims=True) + EPSILON)
    h2 = (residual * scale_two * gain_two).astype(BF)
    h2_stage[...] = h2
    plane_h.start()
    logits = dot(h2, weight(QKV + D, PACKED)).T[:EXPERTS, :]
    highest = jnp.max(jnp.where(routed > 0.5, logits, MASKED), 0, keepdims=True)
    raised = jnp.where(routed > 0.5, jnp.exp(jnp.minimum(logits - highest, 0.0)), 0.0)
    gate = raised / jnp.sum(raised, 0, keepdims=True)
    gate_ref[...] = gate
    for g in range(PLANE):
        info_stage[g, 0:E, :] = slot[g * E : g * E + E, :]
        info_stage[g, E : 2 * E, :] = gate[g * E : g * E + E, :]
    infos = []
    for m in range(1, PLANE):
        g = h.member(m)
        infos.append(
            (remote(info_stage.at[g], info_out.at[h.g], i_s.at[m], i_r.at[m], h.dev(g)),
             remote(info_out.at[g], info_out.at[g], i_s.at[m], i_r.at[m], h.dev(g)))
        )
        infos[-1][0].start()
    mine = [
        pltpu.make_async_copy(info_stage.at[h.g], info_out.at[h.g], loc.at[5]),
        pltpu.make_async_copy(h2_stage, h2_out.at[h.g], loc.at[6]),
    ]
    for c in mine:
        c.start()
    plane_g.third()
    plane_h.second()
    plane_h.third()
    for el in (2, 3):
        for s in range(1, n - 1):
            lines[el].step(s)
    plane_g.fin()
    plane_h.fin()
    for c, landed in infos:
        landed.wait_recv()
    for line in lines:
        line.fin()
    for c in mine:
        c.wait()
    keep.wait()
    line_a.drain()
    plane_a.drain()
    plane_g.drain()
    plane_h.drain()
    for line in lines:
        line.drain()
    for el in range(E):
        mates.drain(el)
    for c, _ in infos:
        c.wait_send()


def first(t, x, routes_t, doc_row, doc_col, counts, cosine, sine_a, sine_b, g, packed, gu, down):
    length = x.shape[0]
    E, n = t.experts, t.n
    shape = jax.ShapeDtypeStruct
    aw_shape = (n, t.f, t.parts, t.part, PACKED)
    return pl.pallas_call(
        functools.partial(first_kernel, t),
        out_shape=(
            shape((E, n, t.piece, D), BF),
            shape((PLANE, length, D), BF),
            shape((PLANE, length, D), BF),
            shape((PLANE, 2 * E, length), F32),
            shape(aw_shape, BF),
            shape((length, D), F32),
            shape((length, H * HD), BF),
            shape((KVH, length, 128), BF),
            shape((KVH, length, HD), BF),
            shape((KVH, length, HD), BF),
            shape((KVH, 2 * length, length), BF),
            shape((EXPERTS, length), F32),
        ),
        in_specs=[VMEM] * 8 + [HBM] * 4,
        out_specs=(HBM, HBM, HBM, HBM, HBM, VMEM, VMEM, VMEM, VMEM, VMEM, HBM, VMEM),
        scratch_shapes=[
            pltpu.VMEM(aw_shape, BF),
            pltpu.VMEM((length, length), F32),
            pltpu.VMEM((2, 2 * length, length), BF),
            pltpu.VMEM((length, D), BF),
            pltpu.VMEM((PLANE, 2 * E, length), F32),
            DMA((8,)),
            DMA((1,)),
            DMA((1,)),
            DMA((2, n)),
            DMA((n,)),
            DMA((9,)),
            DMA((9,)),
            DMA((E, 2)),
            DMA((E, 2)),
            DMA((E, 2, n)),
            DMA((E, n)),
            DMA((9,)),
            DMA((9,)),
            DMA((9,)),
            DMA((9,)),
            DMA((8,)),
            DMA((8,)),
            DMA((2,)),
        ],
        compiler_params=pltpu.CompilerParams(
            collective_id=1, has_side_effects=True, vmem_limit_bytes=LIMIT
        ),
        cost_estimate=pl.CostEstimate(flops=12 * 10**9, bytes_accessed=60 * 2**20, transcendentals=5 * 10**6),
        name="attention_forward",
    )(x, routes_t, doc_row, doc_col, counts, cosine, sine_a, sine_b, g, packed, gu, down)


class LineReduce:
    def __init__(self, here, own, buf, ss, rs):
        self.h, self.own, self.buf, self.ss, self.rs = here, own, buf, ss, rs

    def slot(self, way, d, r):
        return d - r if way == 0 else self.h.t.n - r + d

    def serve(self, way, d):
        h, n = self.h, self.h.t.n
        r = h.r
        to = r + 1 if way == 0 else r - 1
        target = self.buf(self.slot(way, d, to))
        began = (r == 0) if way == 0 else (r == n - 1)

        def begin():
            remote(self.own(d), target, self.ss(way, d), self.rs(way, d), h.dev(h.g, to)).start()

        def go_on():
            here = self.buf(self.slot(way, d, r))
            c = remote(here, target, self.ss(way, d), self.rs(way, d), h.dev(h.g, to))
            remote(here, here, self.ss(way, d), self.rs(way, d), h.dev(h.g, to)).wait_recv()
            here[...] = (here[...].astype(F32) + self.own(d)[...].astype(F32)).astype(BF)
            c.start()

        pl.when(began)(begin)
        pl.when(jnp.logical_not(began))(go_on)

    def turn(self, k):
        h, n = self.h, self.h.t.n
        r = h.r
        j = k - r
        d = n - 1 - j
        pl.when((j >= 0) & (d > r))(lambda: self.serve(0, d))
        j2 = k - (n - 1 - r)
        pl.when((j2 >= 0) & (j2 < r))(lambda: self.serve(1, j2))

    def fin(self):
        h, n = self.h, self.h.t.n
        r = h.r
        mine = self.own(r)

        def add(way):
            here = self.buf(self.slot(way, r, r))
            remote(here, here, self.ss(way, r), self.rs(way, r), h.dev(h.g, r)).wait_recv()
            mine[...] = (here[...].astype(F32) + mine[...].astype(F32)).astype(BF)

        pl.when(r > 0)(lambda: add(0))
        pl.when(r < n - 1)(lambda: add(1))

    def drain(self):
        h, n = self.h, self.h.t.n
        r = h.r
        for d in range(n):
            c = [
                remote(self.own(d), self.buf(0), self.ss(way, d), self.rs(way, d), h.dev(h.g, r))
                for way in (0, 1)
            ]
            pl.when(d > r)(c[0].wait_send)
            pl.when(d < r)(c[1].wait_send)


def second_kernel(
    t,
    info_ref, w_in, h2_in, g_in,
    y_out, row_out, dgate_out, gu_out, down_out,
    w, xs, dj, hid, dy, h2_buf, g_buf, y_stage, row_stage, grads, landed, dg,
    w_sem, in_sem, out_sem, ls, lr, mate_s, mate_r, loc, d_s, d_r,
):
    h = Here(t)
    n, r, sub, E = t.n, h.r, h.sub, t.experts
    h.barrier()
    length = h2_in.shape[1]
    gu_piece, down_piece = t.f * t.rows, t.f * t.rows_down
    dg[...] = jnp.zeros_like(dg)

    def load(step, k):
        s = step % PLANE
        return (
            pltpu.make_async_copy(h2_in.at[s], h2_buf.at[k], in_sem.at[0, k]),
            pltpu.make_async_copy(g_in.at[s], g_buf.at[k], in_sem.at[1, k]),
        )

    def stores(el, s, k):
        return (
            pltpu.make_async_copy(y_stage.at[k], y_out.at[s, el], out_sem.at[0, k]),
            pltpu.make_async_copy(row_stage.at[k], row_out.at[s, el], out_sem.at[1, k]),
        )

    def reducer(el):
        return LineReduce(
            h,
            lambda p: grads.at[el, p],
            lambda k: landed.at[el, k],
            lambda way, p: ls.at[el, way, p],
            lambda way, p: lr.at[el, way, p],
        )

    turns = 2 * (n - 1)

    def serve(tau):
        for el in range(E):
            k = tau - 2 * (el + 1)
            pl.when((k >= 0) & (k < turns))(lambda k=k, el=el: reducer(el).turn(k))

    for c in load(0, 0):
        c.start()
    slots = lax.broadcasted_iota(jnp.int32, (CAP, length), 0).astype(F32)

    def expert(el, carry):
        fetch = pltpu.make_async_copy(w_in.at[el], w, w_sem.at[0])
        fetch.start()
        fetch.wait()

        def sequence(s, carry):
            step = el * PLANE + s
            k = s % 2

            @pl.when(step + 1 < E * PLANE)
            def _():
                for c in load(step + 1, 1 - k):
                    c.start()

            for c in load(step, k):
                c.wait()
            slot_row = info_ref[s, pl.ds(el, 1), :]
            gate_row = info_ref[s, pl.ds(E + el, 1), :]
            hit = slots == slot_row
            pick = jnp.where(hit, 1.0, 0.0).astype(BF)
            gate = jnp.sum(jnp.where(hit, gate_row, 0.0), 1, keepdims=True)
            rows = pl.ds(pl.multiple_of(s * CAP, CAP), CAP)
            x = dot(pick, h2_buf[k]).astype(BF)
            xs[rows, :] = x
            g = dot(pick, g_buf[k])
            d_out = (gate * g).astype(BF)
            dy[rows, :] = d_out
            w_gu = w[:, 0:gu_piece, :].reshape(D, 2 * FF)
            w_down = w[:, gu_piece : gu_piece + down_piece, :].reshape(FF, D)
            joined = dot(x, w_gu)
            gate_pre, up_pre = joined[:, :FF], joined[:, FF:]
            sigmoid = jax.nn.sigmoid(gate_pre)
            active = gate_pre * sigmoid
            hidden = (active * up_pre).astype(BF)
            hid[rows, :] = hidden
            y = dot(hidden, w_down)
            d_gate = jnp.sum(g * y, 1, keepdims=True)
            dg[s, pl.ds(el, 1), :] = jnp.sum(jnp.where(hit, d_gate, 0.0), 0, keepdims=True)

            @pl.when(step >= 2)
            def _():
                for c in stores(el, s, k):
                    c.wait()

            y_stage[k] = (gate * y).astype(BF)
            d_hidden = dot_nt(d_out, w_down)
            d_joined = jnp.concatenate(
                [
                    d_hidden * up_pre * sigmoid * (1.0 + gate_pre * (1.0 - sigmoid)),
                    d_hidden * active,
                ],
                1,
            ).astype(BF)
            dj[rows, :] = d_joined
            row_stage[k] = dot_nt(d_joined, w_gu).astype(BF)
            for c in stores(el, s, k):
                c.start()
            for turn in range(2):
                pl.when(s == 4 * turn + 2)(lambda: serve(2 * el + turn))
            return carry

        lax.fori_loop(0, PLANE, sequence, 0)

        def tile(i, carry):
            cols = pl.ds(pl.multiple_of(i * 256, 256), 256)
            part = dot_tn(xs[:, cols], dj[...]).astype(BF)
            many = 256 * n // D
            if many <= 1:
                grads[el, i // (D // 256 // n), pl.ds(0, 256), :] = part
            else:
                grads[el, pl.ds(i * many, many), 0:gu_piece, :] = part.reshape(many, gu_piece, 2 * FF)
            return carry

        lax.fori_loop(0, D // 256, tile, 0)

        def tile_down(i, carry):
            cols = pl.ds(pl.multiple_of(i * 256, 256), 256)
            part = dot_tn(hid[:, cols], dy[...]).astype(BF)
            many = 256 * n // FF
            grads[el, pl.ds(i * many, many), gu_piece : gu_piece + down_piece, :] = part.reshape(
                many, down_piece, D
            )
            return carry

        lax.fori_loop(0, FF // 256, tile_down, 0)
        return carry

    lax.fori_loop(0, E, expert, 0)
    for k in range(2):
        for c in stores(E - 1, PLANE - 2 + k, k):
            c.wait()
    sends = []
    for m in range(1, PLANE):
        g = h.member(m)
        sends.append(
            (remote(dg.at[g], dgate_out.at[h.g], d_s.at[m], d_r.at[m], h.dev(g)),
             remote(dgate_out.at[g], dgate_out.at[g], d_s.at[m], d_r.at[m], h.dev(g)))
        )
        sends[-1][0].start()
    mine = [pltpu.make_async_copy(dg.at[h.g], dgate_out.at[h.g], loc.at[0])]
    mine[0].start()

    other = t.f - 1 - sub
    parts = lambda s: (pl.ds(s * t.rows, t.rows), pl.ds(gu_piece + s * t.rows_down, t.rows_down))
    mates = Mates(
        h,
        lambda el: [
            (grads.at[el, r, parts(other)[0]], gu_out.at[sub * E + el], gu_out.at[other * E + el]),
            (grads.at[el, r, parts(other)[1]], down_out.at[sub * E + el], down_out.at[other * E + el]),
        ],
        lambda el, k: mate_s.at[el, k],
        lambda el, k: mate_r.at[el, k],
    )
    for tau in range(2 * E, 2 * E + turns):
        serve(tau)
        for el in range(E):
            if tau == 2 * (el + 1) + turns - 1 or (tau == 2 * E and 2 * (el + 1) + turns - 1 < 2 * E):
                reducer(el).fin()
                mates.start(el)
                for k, (src, dst) in enumerate(
                    (
                        (grads.at[el, r, parts(sub)[0]], gu_out.at[sub * E + el]),
                        (grads.at[el, r, parts(sub)[1]], down_out.at[sub * E + el]),
                    )
                ):
                    mine.append(pltpu.make_async_copy(src, dst, loc.at[1 + 2 * el + k]))
                    mine[-1].start()
    for el in range(E):
        mates.wait(el)
    for _, c in sends:
        c.wait_recv()
    for c in mine:
        c.wait()
    for el in range(E):
        reducer(el).drain()
        mates.drain(el)
    for c, _ in sends:
        c.wait_send()


def second(t, info, w, h2, g):
    length = h2.shape[1]
    E, n = t.experts, t.n
    shape = jax.ShapeDtypeStruct
    return pl.pallas_call(
        functools.partial(second_kernel, t),
        out_shape=(
            shape((PLANE, E, CAP, D), BF),
            shape((PLANE, E, CAP, D), BF),
            shape((PLANE, 2 * E, length), F32),
            shape((t.f * E, t.rows, 2 * FF), BF),
            shape((t.f * E, t.rows_down, D), BF),
        ),
        in_specs=[VMEM] + [HBM] * 3,
        out_specs=(HBM,) * 5,
        scratch_shapes=[
            pltpu.VMEM((n, t.piece, D), BF),
            pltpu.VMEM((PLANE * CAP, D), BF),
            pltpu.VMEM((PLANE * CAP, 2 * FF), BF),
            pltpu.VMEM((PLANE * CAP, FF), BF),
            pltpu.VMEM((PLANE * CAP, D), BF),
            pltpu.VMEM((2, length, D), BF),
            pltpu.VMEM((2, length, D), BF),
            pltpu.VMEM((2, CAP, D), BF),
            pltpu.VMEM((2, CAP, D), BF),
            pltpu.VMEM((E, n, t.piece, D), BF),
            pltpu.VMEM((E, n + 1, t.piece, D), BF),
            pltpu.VMEM((PLANE, 2 * E, length), F32),
            DMA((1,)),
            DMA((2, 2)),
            DMA((2, 2)),
            DMA((E, 2, n)),
            DMA((E, 2, n)),
            DMA((E, 2)),
            DMA((E, 2)),
            DMA((1 + 2 * E,)),
            DMA((PLANE,)),
            DMA((PLANE,)),
        ],
        compiler_params=pltpu.CompilerParams(
            collective_id=2, has_side_effects=True, vmem_limit_bytes=LIMIT
        ),
        cost_estimate=pl.CostEstimate(flops=110 * 10**9, bytes_accessed=200 * 2**20, transcendentals=5 * 10**6),
        name="experts",
    )(info, w, h2, g)


def third_kernel(
    t,
    info_ref, y_in, row_in,
    y_out, row_out,
    ybuf, rbuf, stage, from_core, own, near1, near2, last, in_sem, cs, cr, ns, nr,
):
    h = Here(t)
    h.barrier(line=False)
    E = t.experts
    length = stage.shape[2]
    half = length // 2
    order = [(core, b1, b2) for core in (1, 0) for b1, b2 in ((1, 1), (1, 0), (0, 1), (0, 0))]

    def target(i):
        g = h.g
        for on, bit in zip(order[i], (h.core, h.b1, h.b2)):
            if on:
                g = flip(g, bit)
        return g

    def load(i):
        g = target(i)
        k = i % 2
        return (
            pltpu.make_async_copy(row_in.at[g], rbuf.at[k], in_sem.at[0, k]),
            pltpu.make_async_copy(y_in.at[g], ybuf.at[k], in_sem.at[1, k]),
        )

    lanes = lax.broadcasted_iota(jnp.int32, (length, CAP), 1).astype(F32)

    def near(tensor, way, k, src, peer):
        buf = (near1, near2)[way]
        return remote(src, buf.at[tensor, k], ns.at[tensor, way, k], nr.at[tensor, way, k], h.dev(peer))

    def arrived(tensor, way, k):
        buf = (near1, near2)[way].at[tensor, k]
        remote(buf, buf, ns.at[tensor, way, k], nr.at[tensor, way, k], h.dev(h.pc)).wait_recv()
        return (near1, near2)[way][tensor, k].astype(F32)

    for c in load(0):
        c.start()
    lo, hi = pl.ds(0, half), pl.ds(half, half)
    sent = []
    for i in range(8):
        if i < 7:
            for c in load(i + 1):
                c.start()
        columns = info_ref[target(i)].T
        spread = jnp.concatenate(
            [jnp.where(lanes == columns[:, el : el + 1], 1.0, 0.0).astype(BF) for el in range(E)], 1
        )
        for tensor in range(2):
            load(i)[tensor].wait()
            rows = (rbuf, ybuf)[tensor][i % 2].reshape(E * CAP, D)
            block = dot(spread, rows)
            j = i % 4
            if i < 4:
                stage[tensor, j] = block.astype(BF)
                c = remote(
                    stage.at[tensor, j], from_core.at[tensor, j], cs.at[tensor, j], cr.at[tensor, j], h.dev(h.pc)
                )
                c.start()
                sent.append(c)
                continue
            remote(
                from_core.at[tensor, j], from_core.at[tensor, j], cs.at[tensor, j], cr.at[tensor, j], h.dev(h.pc)
            ).wait_recv()
            own[tensor, j] = (block + from_core[tensor, j].astype(F32)).astype(BF)
            whole = own.at[tensor, j]
            if j == 0:
                new = [near(tensor, 0, 0, whole.at[lo], h.p1), near(tensor, 1, 0, whole.at[hi], h.p2)]
            elif j == 1:
                new = [near(tensor, 0, 1, whole.at[lo], h.p1)]
            elif j == 2:
                new = [near(tensor, 1, 1, whole.at[hi], h.p2)]
            else:
                new = []
            for c in new:
                c.start()
            sent += new
    for tensor in range(2):
        own[tensor, 1, hi] = (own[tensor, 1, hi].astype(F32) + arrived(tensor, 1, 0)).astype(BF)
        own[tensor, 2, lo] = (own[tensor, 2, lo].astype(F32) + arrived(tensor, 0, 0)).astype(BF)
        new = [
            near(tensor, 0, 2, own.at[tensor, 1, hi], h.p1),
            near(tensor, 1, 2, own.at[tensor, 2, lo], h.p2),
        ]
        for c in new:
            c.start()
        sent += new
    for tensor, out in ((0, row_out), (1, y_out)):
        out[lo, :] = own[tensor, 3, lo].astype(F32) + arrived(tensor, 0, 1) + arrived(tensor, 1, 2)
        out[hi, :] = own[tensor, 3, hi].astype(F32) + arrived(tensor, 1, 1) + arrived(tensor, 0, 2)
    for c in sent:
        c.wait_send()


def third(t, info, y, rows):
    length = info.shape[2]
    E = t.experts
    shape = jax.ShapeDtypeStruct
    return pl.pallas_call(
        functools.partial(third_kernel, t),
        out_shape=(shape((length, D), F32), shape((length, D), F32)),
        in_specs=[VMEM, HBM, HBM],
        out_specs=(VMEM, VMEM),
        scratch_shapes=[
            pltpu.VMEM((2, E, CAP, D), BF),
            pltpu.VMEM((2, E, CAP, D), BF),
            pltpu.VMEM((2, 4, length, D), BF),
            pltpu.VMEM((2, 4, length, D), BF),
            pltpu.VMEM((2, 4, length, D), BF),
            pltpu.VMEM((2, 3, length // 2, D), BF),
            pltpu.VMEM((2, 3, length // 2, D), BF),
            pltpu.VMEM((8, 128), F32),
            DMA((2, 2)),
            DMA((2, 4)),
            DMA((2, 4)),
            DMA((2, 2, 3)),
            DMA((2, 2, 3)),
        ],
        compiler_params=pltpu.CompilerParams(
            collective_id=3, has_side_effects=True, vmem_limit_bytes=LIMIT
        ),
        cost_estimate=pl.CostEstimate(flops=17 * 10**9, bytes_accessed=40 * 2**20, transcendentals=0),
        name="combine",
    )(info, y, rows)


def rotary_tables(length):
    halfway = HD // 2
    exponent = jnp.arange(halfway, dtype=F32) * (2.0 / HD)
    angles = jnp.arange(length, dtype=F32)[:, None] * (ROTARY_BASE ** (-exponent))[None, :]
    cosine, sine, none = jnp.cos(angles), jnp.sin(angles), jnp.zeros_like(angles)
    return (
        jnp.concatenate([cosine] * 4, -1),
        jnp.concatenate([-sine, none, -sine, none], -1),
        jnp.concatenate([none, sine, none, sine], -1),
    )


def rotate(values, cosine, sine):
    halfway = values.shape[-1] // 2
    turned = jnp.concatenate([-values[..., halfway:], values[..., :halfway]], -1)
    return values * cosine[:, None, :] + turned * sine[:, None, :]


def local(
    t,
    tokens, cotangent, routes, segments, tile_counts, norm1_gain, w_query, w_key, w_value, w_out,
    norm2_gain, w_router, w_gate_up, w_down,
):
    length = tokens.shape[0]
    groups = H // KVH
    highest = lax.Precision.HIGHEST
    rows = t.rows
    packed = jnp.concatenate(
        [
            w_query, w_key, w_value, w_out, w_router, norm1_gain[:, None], norm2_gain[:, None],
            jnp.zeros((rows, PACKED - QKV - D - EXPERTS - 2), BF),
        ],
        1,
    )
    cosine, sine_a, sine_b = rotary_tables(length)
    counts = jnp.broadcast_to(tile_counts.reshape(EXPERTS, 1).astype(F32), (EXPERTS, length))
    (
        w_all, g_all, h2_all, info, packed_all, residual, attended_low, q_all, k_all, v_all, p_all, gating
    ) = first(
        t, tokens, routes.T, segments, segments.reshape(length, 1), counts, cosine, sine_a, sine_b,
        cotangent, packed, w_gate_up, w_down,
    )
    y_slots, row_slots, dgate_all, joined_share, down_share = second(t, info, w_all, h2_all, g_all)
    y_sum, row_sum = third(t, info, y_slots, row_slots)

    full = packed_all.reshape(D, PACKED)
    query_weight = full[:, : H * HD]
    key_weight = full[:, H * HD : H * HD + KVH * HD]
    value_weight = full[:, H * HD + KVH * HD : QKV]
    output_weight = full[:, QKV : QKV + D]
    router_weight = full[:, QKV + D : QKV + D + EXPERTS]
    gain_one = full[:, QKV + D + EXPERTS].astype(F32)
    gain_two = full[:, QKV + D + EXPERTS + 1].astype(F32)
    inputs = tokens.astype(F32)
    upstream = cotangent.astype(F32)
    scale_first = lax.rsqrt(jnp.mean(inputs * inputs, -1, keepdims=True) + EPSILON)
    normed_low = (inputs * scale_first * gain_one).astype(BF)
    scale_second = lax.rsqrt(jnp.mean(residual * residual, -1, keepdims=True) + EPSILON)
    mixed_low = (residual * scale_second * gain_two).astype(BF)
    cosine, sine = cosine[:, :HD], (sine_b - sine_a)[:, :HD]
    query_low = q_all.reshape(KVH, length, groups, HD).transpose(1, 0, 2, 3)
    key_low = k_all.transpose(1, 0, 2)
    value_low = v_all.transpose(1, 0, 2)
    output = (residual + y_sum).astype(BF)
    gating_grad = dgate_all[:, : t.experts].reshape(EXPERTS, length)
    chosen_grad = gating * (gating_grad - jnp.sum(gating * gating_grad, 0, keepdims=True))
    logits_grad = chosen_grad.T
    router_grad = jnp.dot(mixed_low.astype(F32).T, logits_grad, precision=highest)
    mixed_grad = jnp.dot(logits_grad, router_weight.astype(F32).T, precision=highest) + row_sum
    gained_two = gain_two * mixed_grad
    gain_two_grad = jnp.sum(mixed_grad * residual * scale_second, 0)
    residual_grad = (
        upstream
        + scale_second * gained_two
        - residual * scale_second**3 * jnp.mean(gained_two * residual, -1, keepdims=True)
    )
    branch_low = residual_grad.astype(BF)
    output_weight_grad = jnp.einsum("sn,sm->nm", attended_low, branch_low, preferred_element_type=F32)
    attended_grad = jnp.einsum("sm,nm->sn", branch_low, output_weight, preferred_element_type=F32)
    attended_grad = attended_grad.astype(BF).reshape(length, KVH, groups, HD)
    probs_again = p_all.reshape(KVH, groups, length, length)
    probs = probs_again.astype(F32)
    value_grad = jnp.einsum("kgqt,qkgd->tkd", probs_again, attended_grad, preferred_element_type=F32)
    probs_grad = jnp.einsum("qkgd,tkd->kgqt", attended_grad, value_low, preferred_element_type=F32)
    scores_grad = (probs * (probs_grad - jnp.sum(probs * probs_grad, -1, keepdims=True))).astype(BF)
    query_grad = jnp.einsum("kgqt,tkd->qkgd", scores_grad, key_low, preferred_element_type=F32).reshape(
        length, H, HD
    ) * HD ** (-0.5)
    key_grad = jnp.einsum("kgqt,qkgd->tkd", scores_grad, query_low, preferred_element_type=F32) * HD ** (-0.5)
    query_back = rotate(query_grad, cosine, -sine).astype(BF).reshape(length, H * HD)
    key_back = rotate(key_grad, cosine, -sine).astype(BF).reshape(length, KVH * HD)
    value_back = value_grad.astype(BF).reshape(length, KVH * HD)
    query_weight_grad = jnp.einsum("sm,sn->mn", normed_low, query_back, preferred_element_type=F32)
    key_weight_grad = jnp.einsum("sm,sn->mn", normed_low, key_back, preferred_element_type=F32)
    value_weight_grad = jnp.einsum("sm,sn->mn", normed_low, value_back, preferred_element_type=F32)
    normed_grad = jnp.einsum("sn,mn->sm", query_back, query_weight, preferred_element_type=F32)
    normed_grad = normed_grad + jnp.einsum("sn,mn->sm", key_back, key_weight, preferred_element_type=F32)
    normed_grad = normed_grad + jnp.einsum("sn,mn->sm", value_back, value_weight, preferred_element_type=F32)
    gained_one = gain_one * normed_grad
    gain_one_grad = jnp.sum(normed_grad * inputs * scale_first, 0)
    token_grad = (
        residual_grad
        + scale_first * gained_one
        - inputs * scale_first**3 * jnp.mean(gained_one * inputs, -1, keepdims=True)
    )
    summed = lax.psum(
        (
            gain_one_grad, query_weight_grad, key_weight_grad, value_weight_grad, output_weight_grad,
            gain_two_grad, router_grad,
        ),
        ("expert", "shard"),
    )
    member = lax.axis_index("shard")
    shares = tuple(
        lax.dynamic_slice_in_dim(total, member * (total.shape[0] // t.shards), total.shape[0] // t.shards, 0)
        for total in summed
    )
    return (output, token_grad) + shares + (joined_share.astype(F32), down_share.astype(F32))


def solution(mesh):
    both, rows, held = P(("expert", "shard"), None), P("shard", None), P("expert", "shard", None)
    in_specs = (both,) * 5 + (P("shard"), rows, rows, rows, rows, P("shard"), rows, held, held)
    out_specs = (both, both, P("shard"), rows, rows, rows, rows, P("shard"), rows, held, held)
    return jax.shard_map(
        functools.partial(local, Sizes(mesh)), mesh=mesh, in_specs=in_specs, out_specs=out_specs, check_vma=False
    )
```

time: 1950 us -> 969 us (0.50)
  waiting for transfers between devices: 1090 us -> 177 us
  Pallas kernels: 0 us -> 620 us
  blocking collectives: 298 us -> 40.6 us
  matrix products: 220 us -> 42.8 us
  local copies, waits for them, and re-layouts: 161 us -> 38.4 us
  other arithmetic: 135 us -> 26.6 us
  starting transfers between devices: 21.8 us -> 0.04 us
    pallas_call x0 -> x3, Pallas kernels: none -> 620 us  [the longest x1 266 us: first(): pl.pallas_call(functools.partial(first_kernel, t), out_shape=(shape((E, n...]
    all_to_all x3 -> x0, waiting for transfers between devices: 502 us -> none  [the longest x1 182 us: local(): lax.all_to_all(outgoing, 'expert', split_axis=0, concat_axis=0, tiled=True)]
    reduce_scatter x2 -> x0, waiting for transfers between devices: 280 us -> none  [the longest x1 280 us: local(): lax.psum_scatter(joined_weight_grad.astype(jnp.bfloat16), 'shard', scatte...]
    all_to_all x1 -> x0, blocking collectives: 194 us -> none  [local(): lax.all_to_all(outgoing_grad, 'expert', split_axis=0, concat_axis=0, tile...]
    dot_general x19 -> x6, matrix products: 182 us -> 14.3 us  [the longest x1 3.41 us: local(): jnp.einsum('sm,sn->mn', normed_low, query_back, preferred_element_type=F32)]
    all_gather x6 -> x0, waiting for transfers between devices: 149 us -> none  [the longest x1 54.8 us: local(): lax.all_gather(w_down, 'shard', axis=1, tiled=True)]
    all_gather x3 -> x0, blocking collectives: 65.2 us -> none  [the longest x1 26.4 us: local(): lax.all_gather(w_router, 'shard', axis=0, tiled=True)]
    scatter x1 -> x0, local copies, waits for them, and re-layouts: 57.9 us -> none  [local(): jnp.zeros((EXPERTS * CAP, D), jnp.bfloat16).at[target]]
  transfers between devices with their start and end apart: 12 -> 1, of which waited for: 9 -> 1; matrix products, arithmetic and copies ran while one was open for 17% -> 2% of each run, Pallas kernels for 0% -> 0%
where the time goes in v1:
time: 969 us; the launch traced here: 960 us
  Pallas kernels  620 us (64%)
  waiting for transfers between devices  177 us (18%)
  matrix products  42.8 us (4%)
  blocking collectives  40.6 us (4%)
  local copies, waits for them, and re-layouts  38.4 us (4%)
  other arithmetic  26.6 us (3%)
  between operations  14.7 us (2%)
    pallas_call x1, Pallas kernels, first(): pl.pallas_call(functools.partial(first_kernel, t), out_shape=(shape((E, n...  266 us
    pallas_call x1, Pallas kernels, second(): pl.pallas_call(functools.partial(second_kernel, t), out_shape=(shape((PLA...  264 us
    psum x1, waiting for transfers between devices, local(): lax.psum((gain_one_grad, query_weight_grad, key_weight_grad, value_weight...  177 us
    pallas_call x1, Pallas kernels, third(): pl.pallas_call(functools.partial(third_kernel, t), out_shape=(shape((leng...  89.8 us
    psum x1, blocking collectives, local(): lax.psum((gain_one_grad, query_weight_grad, key_weight_grad, value_weight...  40.6 us
  transfers between devices with their start and end apart: 1, of which 1 were waited for; matrix products, arithmetic and copies ran while one was open for 2% of the time, Pallas kernels for 0%

profile of v1, /device:TPU:0, one launch (start us, length us, event | category | flops | bytes accessed | tf_op | source)
XLA Modules:
  0.0 959.8 jit_solution(3931509147972549540)
XLA Ops:
  7.2 0.7 convert_bitcast_fusion
  7.9 1.5 fusion.2
  9.4 0.6 multiply_multiply_fusion
  10.0 0.8 copy.58
  10.8 0.8 copy.59
  11.6 0.8 copy.57
  12.4 1.5 copy.60.doc_col_ref
  13.9 1.0 fusion.37
  15.0 0.1 maximum_multiply_fusion.2
  15.1 0.8 copy.69
  15.9 1.4 pad_maximum_fusion.2
  17.3 0.8 copy.70
  18.1 1.1 concatenate.24.packed_in
  19.2 0.7 broadcast_in_dim.10.counts_ref
  19.9 265.9 %attention_forward.1 = (bf16[4,4,384,1024]{3,2,1,0:T(8,128)(2,1)}, bf16[8,512,1024]{2,1,0:T(8,128)(2,1)}, bf16[8,512,1024]{2,1,0:T(8,128)(2,1)}, f32[8,8,512]{2,...) custom-call(bf16[512,1024]{1,0:T(8,128)(2,1)} %x_ref.1, ...), custom_call_target="tpu_custom_call" | custom-call | flops 12000000000 | bytes 62914560 | tf_op jit(solution)/shard_map/attention_forward/pallas_call | solution.py:493
  285.8 1.9 multiply_reduce_fusion.2
  287.7 1.3 copy.71
  289.1 1.3 slice_convert_fusion
  290.4 0.8 copy.88
  291.2 0.2 copy.87
  291.3 264.0 %experts.1 = (bf16[8,4,256,1024]{3,2,1,0:T(8,128)(2,1)}, bf16[8,4,256,1024]{3,2,1,0:T(8,128)(2,1)}, f32[8,8,512]{2,1,0:T(8,128)}, bf16[8,128,1024]{2,1,0:T(8,128)(2,1)}, bf16[8,64,1024]{2,1,0:T(8,128)(2,1)}) custom-call(f32[8,8,512]{2,1,0:T(8,128)} %get-tuple-element.31.info_ref, bf16[4,4,384,1024]{3,2,1,0:T(8,128)(2,1)} %get-tuple-element.32.w_in, ...), custom_call_target="tpu_custom_call" | custom-call | flops 109999996928 | bytes 209715200 | tf_op jit(solution)/shard_map/experts/pallas_call | solution.py:796
  555.3 0.9 slice.42
  556.3 89.8 %combine.1 = (f32[512,1024]{1,0:T(8,128)}, f32[512,1024]{1,0:T(8,128)}) custom-call(f32[8,8,512]{2,1,0:T(8,128)} %get-tuple-element.31.info_ref, bf16[8,4,256,1024]{3,2,1,0:T(8,128)(2,1)} %get-tuple-element.35.y_in, bf16[8,4,256,1024]{3,2,1,0:T(8,128)(2,1)} %get-tuple-element.36.row_in), custom_call_target="tpu_custom_call" | custom-call | flops 16999999488 | bytes 41943040 | tf_op jit(solution)/shard_map/combine/pallas_call | solution.py:940
  646.1 1.4 fusion.20
  647.6 0.1 copy-done.12
  647.7 2.7 multiply_reduce_fusion
  650.5 1.7 multiply_subtract_fusion
  652.2 1.3 copy-done.3
  653.5 2.9 fusion.16
  656.4 0.5 copy.64
  656.9 12.7 %copy.63 = bf16[8,2,512,512]{2,3,1,0:T(8,128)(2,1)} copy(bf16[8,2,512,512]{3,2,1,0:T(8,128)(2,1)} %bitcast.78) | data formatting | bytes 16777216 | tf_op jit(solution)/shard_map/reshape | solution.py:1048
  669.7 5.8 fusion.19
  675.5 3.4 fusion.32
  679.0 1.4 copy-done
  680.4 3.9 fusion
  684.3 5.8 fusion.1
  690.1 3.9 broadcast_multiply_fusion
  694.1 1.6 bitcast_multiply_fusion.1
  695.7 0.1 slice_negate_fusion.1
  695.8 0.2 slice_negate_fusion
  696.1 0.9 copy-done.2
  697.0 0.1 copy-done.6
  697.1 2.3 fusion.40
  699.4 0.3 fusion.25
  699.7 2.3 fusion.42
  702.0 0.3 maximum_multiply_fusion
  702.3 0.6 fusion.15
  702.9 1.0 copy-done.20
  703.8 3.4 fusion.44
  707.3 2.9 convert_element_type.99
  710.2 2.8 convert_element_type.98
  713.0 2.2 fusion.22
  715.2 2.9 fusion.10
  718.2 3.8 fusion.7
  722.0 40.6 %all-reduce = (f32[1024]{0:T(1024)S(1)}, f32[1024]{0:T(1024)S(1)}) all-reduce(f32[1024]{0:T(1024)S(1)} %get-tuple-element.51, f32[1024]{0:T(1024)S(1)} %get-tuple-element.49), channel_id=1, replica_groups=mesh['expert'=4,'shard'=8] {'expert','shard'}, use_global_device_ids=true, to_apply=%region_7.0 | all-reduce | flops 2048 | bytes 16384 | tf_op jit(solution)/shard_map/psum | solution.py:1073
  762.6 0.6 dynamic_slice.21
  763.2 0.6 dynamic_slice.26
  763.8 3.5 fusion.4
  767.3 177.1 %all-reduce.4.cloned.1.call-done = (f32[1024,1024]{1,0:T(8,128)}, f32[1024,512]{1,0:T(8,128)}, f32[1024,512]{1,0:T(8,128)}, f32[1024,1024]{1,0:T(8,128)}, f32[1024,32]{0,1:T(8,128)}) async-done(((f32[1024,1024]{1,0:T(8,128)}, f32[1024,512]{1,0:T(8,128)}, f32[1024,512]{1,0:T(8,128)}, f32[1024,1024]{1,0:T(8,128)}, f32[1024,32]{0,1:T(8,128)}), (f32[1024,1024]{1,0:T(8,128)}, f32[1024,512]{1,0:T(8,128)}, ...) | async-done | bytes 12714000 | tf_op jit(solution)/shard_map/psum | solution.py:1073
  944.4 1.9 constant_dynamic-slice_fusion.4
  946.2 1.3 constant_dynamic-slice_fusion
  947.6 1.7 constant_dynamic-slice_fusion.3
  949.2 1.7 constant_dynamic-slice_fusion.2
  950.9 1.9 constant_dynamic-slice_fusion.1
  (65 shorter events, 0.3 us)
Async XLA Ops:
  7.2 937.2 %all-reduce.4.cloned.1.call-start = ((), (), s32[]{:S(2)}) async-start(), calls=%async_computation | async-start | bytes 25427968 | tf_op jit(solution)/shard_map/psum | solution.py:1073
  14.9 3.2 copy-start.23
  14.9 3.2 copy-start.24
  14.9 3.2 copy-start.25
  15.0 3.2 copy-start.26
  17.3 2.6 copy-start.17
  17.3 2.6 copy-start.18
  285.8 1.9 copy-start.19
  556.3 89.8 %copy-start.22 = (f32[32,512]{1,0:T(8,128)S(1)}, f32[32,512]{1,0:T(8,128)}, u32[]{:S(2)}) copy-start(f32[32,512]{1,0:T(8,128)} %get-tuple-element.39) | copy-start | bytes 196612
  556.3 89.8 %copy-start.1 = (f32[512,1024]{1,0:T(8,128)S(1)}, f32[512,1024]{1,0:T(8,128)}, u32[]{:S(2)}) copy-start(f32[512,1024]{1,0:T(8,128)} %get-tuple-element.30) | copy-start | bytes 6291460
  646.1 1.6 copy-start.12
  647.7 2.8 copy-start.11
  647.7 2.8 copy-start.16
  652.2 1.3 copy-start.3
  656.9 12.7 %copy-start.5 = (bf16[512,1024]{0,1:T(8,128)(2,1)}, bf16[512,1024]{0,1:T(8,128)(2,1)S(1)}, u32[]{:S(2)}) copy-start(bf16[512,1024]{0,1:T(8,128)(2,1)S(1)} %copy.64) | copy-start | bytes 3145732
  669.7 5.8 copy-start.4
  669.7 5.8 copy-start.9
  675.5 4.9 copy-start
  690.1 4.0 copy-start.13
  695.8 1.2 copy-start.2
  695.8 1.3 copy-start.6
  695.8 1.3 copy-start.27
  695.8 1.3 copy-start.28
  696.1 3.3 copy-start.14
  696.1 3.3 copy-start.15
  699.7 2.3 copy-start.8
  702.9 1.0 copy-start.20
  707.3 2.9 copy-start.10
  713.0 2.2 copy-start.21
  715.2 3.0 copy-start.7
  718.2 45.6 %copy-start.29 = (f32[512]{0:T(512)S(1)}, f32[512]{0:T(512)}, u32[]{:S(2)}) copy-start(f32[512]{0:T(512)} %get-tuple-element.70) | copy-start | bytes 6148
Sparse Core Ops, SparseCore 0:
  707.4 236.9 all-reduce.3
